TPU v7x, 32 devices: a whole 2x2x4 slice. The times are simulated.
32 devices in a mesh: fsdp: 8 (over z, x), tp: 4 (over y, core).
Axes of the slice: x: 2, y: 2, z: 4, core: 2. Of those that a mesh axis runs over, the one named last changes fastest.
Arguments:
- activations: bfloat16 [1024, 5120], P('fsdp', 'tp'), may hold values from -6 to 6
- out_grad: bfloat16 [1024, 5120], P('fsdp'), may hold values from -0.25 to 0.25
- momentum: float32 [5120, 5120], P('fsdp', 'tp'), may hold values from -6 to 6
- right_prev: float32 [5120, 256], P('tp'), may hold values from -6 to 6
Outputs:
- new_momentum: float32 [5120, 5120], P('fsdp', 'tp')
- update: float32 [5120, 5120], P('fsdp', 'tp')
- right_next: float32 [5120, 256], P('tp', 'fsdp')
All inputs are finite; a program needn't handle non-finite values.
Results may differ from a plain program's by a relative error of at most 0.0003.
Values sent between devices are 32-bit elements; how exact they have to be, the bound alone decides.
A program may use at most 128 MiB of HBM per device.

v0:
```python
import math

import jax
import jax.numpy as jnp
from jax import lax
from jax.sharding import PartitionSpec as P

D = 5120
R = 256


momentum_decay = 0.95


def token_product(out_grad, columns_in):
    return lax.dot_general(
        out_grad, columns_in, (((0,), (0,)), ((), ())), preferred_element_type=jnp.float32
    )


def on_device(activations, out_grad, momentum, right_prev):
    high = lax.Precision.HIGHEST
    grad = lax.psum_scatter(
        token_product(out_grad, activations), "fsdp", scatter_dimension=0, tiled=True
    )
    buffer = momentum + grad
    partial_left = jnp.dot(buffer, right_prev, precision=high)
    left = lax.psum(partial_left, "tp")
    gram = lax.psum(jnp.dot(left.T, left, precision=high), "fsdp")
    lower = jnp.linalg.cholesky(gram)
    basis = lax.linalg.triangular_solve(lower, left, left_side=False, lower=True, transpose_a=True)
    partial_right = jnp.dot(buffer.T, basis, precision=high)
    right = lax.psum(partial_right, "fsdp")
    squares = lax.psum(jnp.sum(right * right, axis=0), "tp")
    factor = lax.rsqrt(squares / D + 1e-06)
    right_next = right * factor[None, :]
    new_momentum = buffer - (1.0 - momentum_decay) * jnp.dot(basis, right.T, precision=high)
    update = math.sqrt(D / R) * jnp.dot(basis, right_next.T, precision=high)
    own_columns = right_next.shape[1] // lax.axis_size("fsdp")
    first_column = lax.axis_index("fsdp") * own_columns
    right_owned = lax.dynamic_slice_in_dim(right_next, first_column, own_columns, 1)
    return (new_momentum, update, right_owned)


def solution(mesh):
    return jax.shard_map(
        on_device,
        mesh=mesh,
        in_specs=(P("fsdp", "tp"), P("fsdp", None), P("fsdp", "tp"), P("tp", None)),
        out_specs=(P("fsdp", "tp"), P("fsdp", "tp"), P("tp", "fsdp")),
        check_vma=False,
    )
```

profile of v0, /device:TPU:27, one launch (start us, length us, event | category | flops | bytes accessed | tf_op | source)
XLA Modules:
  0.0 742.1 jit_solution(16822899175458384700)
XLA Ops:
  7.2 1.3 copy-done
  8.5 11.5 %fusion.14 = f32[5120,1280]{1,0:T(8,128)} fusion(bf16[128,5120]{1,0:T(8,128)(2,1)S(1)} %copy-done, bf16[128,1280]{1,0:T(8,128)(2,1)} %param.4), kind=kOutput, calls=%fused_computation.40 | convolution fusion | flops 1677721600 | bytes 27852800 | tf_op jit(solution)/shard_map/dot_general | solution.py:16
  20.1 417.6 %reduce-scatter.2.cloned.1.call-done = f32[640,1280]{1,0:T(8,128)} async-done(((f32[5120,1280]{1,0:T(8,128)}), f32[640,1280]{1,0:T(8,128)}) %reduce-scatter.2.cloned.1.call-update) | async-done | bytes 3276816 | tf_op jit(solution)/shard_map/reduce_scatter | solution.py:23
  437.7 3.3 add.44
  441.0 1.7 copy-done.1
  442.7 3.6 fusion.15
  446.3 33.7 %all-reduce.5.cloned.1.call-done = f32[640,256]{1,0:T(8,128)} async-done(((f32[640,256]{1,0:T(8,128)}), f32[640,256]{1,0:T(8,128)}) %all-reduce.5.cloned.1.call-update) | async-done | bytes 655376 | tf_op jit(solution)/shard_map/psum | solution.py:28
  480.0 3.2 fusion.16
  483.5 68.7 %all-reduce.7.cloned.1.call-done = f32[256,256]{0,1:T(8,128)} async-done(((f32[256,256]{0,1:T(8,128)}), f32[256,256]{0,1:T(8,128)}) %all-reduce.7.cloned.1.call-update) | async-done | bytes 262160 | tf_op jit(solution)/shard_map/psum | solution.py:29
  552.2 1.1 copy.8
  553.3 1.0 fusion.4
  554.3 11.7 %cholesky.50 = f32[128,128]{1,0:T(8,128)S(1)} custom-call(f32[128,128]{1,0:T(8,128)S(1)} %cholesky.118), custom_call_target="Cholesky" | custom-call | tf_op jit(solution)/shard_map/jit(cholesky)/cholesky | solution.py:30
  566.0 9.8 %custom-call.14 = f32[1,128,128]{1,2,0:T(8,128)S(1)} custom-call(f32[1,128,128]{2,1,0:T(8,128)S(1)} %get-tuple-element.27), custom_call_target="InvertDiagBlocksLowerTriangular" | custom-call | tf_op jit(solution)/shard_map/jit(cholesky)/cholesky | solution.py:30
  576.4 11.7 %cholesky.105 = f32[128,128]{1,0:T(8,128)S(1)} custom-call(f32[128,128]{1,0:T(8,128)S(1)} %convolution_subtract_fusion.1), custom_call_target="Cholesky" | custom-call | tf_op jit(solution)/shard_map/jit(cholesky)/cholesky | solution.py:30
  588.1 0.7 compare_reduce_fusion
  590.1 4.1 while.1
  590.4 0.6 fusion.31
  590.9 1.4 bitcast_dynamic-update-slice_fusion.2
  592.3 0.6 fusion.31
  592.9 1.4 bitcast_dynamic-update-slice_fusion.2
  594.3 19.7 %custom-call.15 = f32[2,128,128]{1,2,0:T(8,128)S(1)} custom-call(f32[2,128,128]{2,1,0:T(8,128)S(1)} %get-tuple-element.10), custom_call_target="InvertDiagBlocksLowerTriangular" | custom-call | tf_op jit(solution)/shard_map/triangular_solve | solution.py:31
  614.0 0.5 fusion.2
  614.5 0.7 convolution_subtract_fusion
  615.2 0.5 fusion.5
  615.7 8.3 %fusion.1 = f32[1280,256]{1,0:T(8,128)} fusion(f32[640,1280]{1,0:T(8,128)} %copy-done.1, f32[640,128]{0,1:T(8,128)S(1)} %fusion.5, f32[640,128]{0,1:T(8,128)S(1)} %fusion.2), kind=kOutput, calls=%fused_computation.10 | convolution fusion | flops 2516746240 | bytes 5242880 | tf_op jit(solution)/shard_map/dot_general | solution.py:32
  624.0 84.6 %all-reduce.9.cloned.1.call-done = f32[1280,256]{1,0:T(8,128)} async-done(((f32[1280,256]{1,0:T(8,128)}), f32[1280,256]{1,0:T(8,128)}) %all-reduce.9.cloned.1.call-update) | async-done | bytes 1310736 | tf_op jit(solution)/shard_map/psum | solution.py:33
  708.6 1.6 multiply_reduce_fusion
  710.2 5.9 psum.31
  716.2 7.0 convolution_multiply_fusion
  723.2 1.1 constant_dynamic-slice_fusion.1
  724.3 2.0 copy.9
  726.3 8.9 %fusion = f32[640,1280]{1,0:T(8,128)} fusion(f32[640,1280]{1,0:T(8,128)} %copy-done.1, f32[1280,256]{1,0:T(8,128)S(1)} %copy-done.2, f32[640,128]{0,1:T(8,128)S(1)} %fusion.5, f32[640,128]{0,1:T(8,128)S(1)} %fusion.2), kind=kOutput, calls=%fused_computation.4 | convolution fusion | flops 2518384640 | bytes 8519680 | tf_op jit(solution)/shard_map/dot_general | solution.py:37
  (30 shorter events, 1.2 us)
Async XLA Ops:
  7.2 1.3 copy-start
  7.2 430.5 %reduce-scatter.2.cloned.1.call-start = ((), (), s32[]{:S(2)}) async-start(), calls=%async_computation.1 | async-start | bytes 29491200 | tf_op jit(solution)/shard_map/reduce_scatter | solution.py:23
  20.0 422.7 %copy-start.4 = (f32[1280,256]{1,0:T(8,128)S(1)}, f32[1280,256]{1,0:T(8,128)}, u32[]{:S(2)}) copy-start(f32[1280,256]{1,0:T(8,128)} %param.7) | copy-start | bytes 3932164
  20.0 460.0 %all-reduce.5.cloned.1.call-start = ((), (), s32[]{:S(2)}) async-start(), calls=%async_computation.2 | async-start | bytes 1310720 | tf_op jit(solution)/shard_map/psum | solution.py:28
  441.0 1.7 copy-start.1
  446.3 105.9 %all-reduce.7.cloned.1.call-start = ((), (), s32[]{:S(2)}) async-start(), calls=%async_computation.3 | async-start | bytes 524288 | tf_op jit(solution)/shard_map/psum | solution.py:29
  483.3 225.3 %all-reduce.9.cloned.1.call-start = ((), (), s32[]{:S(2)}) async-start(), calls=%async_computation.4 | async-start | bytes 2621440 | tf_op jit(solution)/shard_map/psum | solution.py:33
  554.3 59.7 %copy-start.3 = (f32[640,256]{1,0:T(8,128)S(1)}, f32[640,256]{1,0:T(8,128)}, u32[]{:S(2)}) copy-start(f32[640,256]{1,0:T(8,128)} %all-reduce.5.cloned.1.call-done) | copy-start | bytes 1966084
  708.6 7.6 %copy-start.2 = (f32[1280,256]{1,0:T(8,128)S(1)}, f32[1280,256]{1,0:T(8,128)}, u32[]{:S(2)}) copy-start(f32[1280,256]{1,0:T(8,128)} %all-reduce.9.cloned.1.call-done) | copy-start | bytes 3932164
Sparse Core Ops, SparseCore 0:
  20.1 417.4 reduce-scatter.1
  446.4 33.5 all-reduce.4
  484.3 67.7 all-reduce.6
  624.1 84.4 all-reduce.8
where the time goes:
time: 752 us; the launch traced here: 742 us
  waiting for transfers between devices  605 us (80%)
  other arithmetic  59.7 us (8%)
  matrix products  44.6 us (6%)
  between operations  15.6 us (2%)
  local copies, waits for them, and re-layouts  11.1 us (1%)
    reduce_scatter x1, waiting for transfers between devices, on_device(): lax.psum_scatter(token_product(out_grad, activations), 'fsdp', scatter_di...  418 us
    psum x1, waiting for transfers between devices, on_device(): right = lax.psum(partial_right, 'fsdp')  84.6 us
    psum x1, waiting for transfers between devices, on_device(): gram = lax.psum(jnp.dot(left.T, left, precision=high), 'fsdp')  68.7 us
    another operation x6, other arithmetic, on_device(): lower = jnp.linalg.cholesky(gram)  34 us
    psum x1, waiting for transfers between devices, on_device(): left = lax.psum(partial_left, 'tp')  33.7 us
    another operation x3, other arithmetic, on_device(): lax.linalg.triangular_solve(lower, left, left_side=False, lower=True, tra...  19.7 us
  transfers between devices with their start and end apart: 4, of which 4 were waited for; matrix products, arithmetic and copies ran while one was open for 0% of the time, Pallas kernels for 0%

commit v1 on v0

v1 whole, which is shorter than its diff:
```python
import functools
import math

import jax
import jax.numpy as jnp
from jax import lax
from jax.experimental import pallas as pl
from jax.experimental.pallas import tpu as pltpu
from jax.sharding import PartitionSpec as P

HIGH = lax.Precision.HIGHEST
F32 = jnp.float32
BF16 = jnp.bfloat16
LANES = 128
PANEL = 8
VMEM_LIMIT = 56 * 1024 * 1024

momentum_decay = 0.95


def dot(a, b, dims=((1,), (0,))):
    return lax.dot_general(a, b, (dims, ((), ())), precision=HIGH, preferred_element_type=F32)


def remote(src, dst, send, recv, device):
    return pltpu.make_async_remote_copy(
        src_ref=src, dst_ref=dst, send_sem=send, recv_sem=recv,
        device_id=device, device_id_type=pl.DeviceIdType.MESH,
    )


def greet(n, m, f, t):
    barrier = pltpu.get_barrier_semaphore()
    for k in range(1, n):
        pl.semaphore_signal(barrier, inc=1, device_id=(lax.rem(f + k, n), t),
                            device_id_type=pl.DeviceIdType.MESH)
    for k in range(1, m):
        pl.semaphore_signal(barrier, inc=1, device_id=(f, lax.rem(t + k, m)),
                            device_id_type=pl.DeviceIdType.MESH)
    pl.semaphore_wait(barrier, n + m - 2)


def main_kernel(n, m, a_ref, g_ref, mom_ref, p_ref,
                buf_ref, left_ref, gram_ref, s_ref,
                agath, ggath, gsend, gt, lpart, lrecv, gpart, grecv, spart, srecv,
                az_send, az_recv, ax_send, ax_recv, gs_send, gs_recv, gt_send, gt_recv,
                l_send, l_recv, l2_send, l2_recv, q_send, q_recv, q2_send, q2_recv,
                s_send, s_recv, s2_send, s2_recv):
    f = lax.axis_index("fsdp")
    t = lax.axis_index("tp")
    nz = n // 2
    z, x = f // 2, lax.rem(f, 2)
    xpeer = z * 2 + (1 - x)
    tok, wide = a_ref.shape
    quarter = tok // m
    rows = mom_ref.shape[0]
    agath[f] = a_ref[...].astype(F32)
    for d in range(n):
        gsend[d] = g_ref[pl.ds(pl.multiple_of(t * quarter, quarter), quarter),
                         d * rows:(d + 1) * rows].astype(F32)
    ggath[f, t] = gsend[f]
    greet(n, m, f, t)

    for k in range(1, n):
        d = lax.rem(f + k, n)
        remote(gsend.at[d], ggath.at[f, t], gs_send.at[k - 1], gs_recv.at[k - 1], (d, t)).start()

    def az(slot, way, k):
        target = (z + 1) * 2 + x if way == 0 else (z - 1) * 2 + x
        sem = slot // 2
        return remote(agath.at[slot], agath.at[slot], az_send.at[way, k], az_recv.at[sem], (target, t))

    def ax(slot):
        return remote(agath.at[slot], agath.at[slot], ax_send.at[slot // 2], ax_recv.at[slot // 2],
                      (xpeer, t))

    pl.when(z < nz - 1)(lambda: az(f, 0, 0).start())
    pl.when(z > 0)(lambda: az(f, 1, 0).start())
    ax(f).start()

    def gather_step(k):
        @pl.when(z >= k)
        def _():
            slot = f - 2 * k
            az(slot, 0, k).wait_recv()
            pl.when(z < nz - 1)(lambda: az(slot, 0, k).start())
            ax(slot).start()

        @pl.when(z + k < nz)
        def _():
            slot = f + 2 * k
            az(slot, 1, k).wait_recv()
            pl.when(z > 0)(lambda: az(slot, 1, k).start())
            ax(slot).start()

    def gs_wait():
        for k in range(1, n):
            source = lax.rem(f - k + n, n)
            remote(gsend.at[f], ggath.at[source, t], gs_send.at[k - 1], gs_recv.at[k - 1],
                   (source, t)).wait_recv()

    gather_step(1)
    gs_wait()
    for k in range(1, m):
        d = lax.rem(t + k, m)
        remote(ggath.at[:, t], ggath.at[:, t], gt_send.at[k - 1], gt_recv.at[k - 1], (f, d)).start()
    for k in range(2, nz):
        gather_step(k)
    for k in range(1, m):
        source = lax.rem(t - k + m, m)
        remote(ggath.at[:, source], ggath.at[:, source], gt_send.at[k - 1], gt_recv.at[k - 1],
               (f, source)).wait_recv()
    gt[...] = ggath[...].reshape(n * tok, rows).astype(BF16).T
    for zz in range(nz):
        slot = 2 * zz + (1 - x)
        remote(agath.at[slot], agath.at[slot], ax_send.at[zz], ax_recv.at[zz], (xpeer, t)).wait_recv()

    tile = 2 * LANES
    for j in range(wide // tile):
        col = slice(j * tile, (j + 1) * tile)
        part = agath[:, :, col].reshape(n * tok, tile).astype(BF16)
        grad = jnp.dot(gt[...], part, preferred_element_type=F32)
        b = mom_ref[:, col] + grad
        buf_ref[:, col] = b
        term = dot(b, p_ref[col, :])
        lpart[...] = term if j == 0 else lpart[...] + term

    share = rows // m
    for k in range(1, m):
        d = lax.rem(t + k, m)
        remote(lpart.at[pl.ds(pl.multiple_of(d * share, share), share)], lrecv.at[k - 1],
               l_send.at[k - 1], l_recv.at[k - 1], (f, d)).start()
    mine = pl.ds(pl.multiple_of(t * share, share), share)
    for k in range(1, m):
        remote(lpart.at[mine], lrecv.at[k - 1], l_send.at[k - 1], l_recv.at[k - 1], (f, t)).wait_recv()
    total = lpart[mine, :]
    for k in range(1, m):
        total = total + lrecv[k - 1]
    left_ref[mine, :] = total
    for k in range(1, m):
        d = lax.rem(t + k, m)
        remote(left_ref.at[mine], left_ref.at[mine], l2_send.at[k - 1], l2_recv.at[k - 1], (f, d)).start()
    for k in range(1, m):
        source = lax.rem(t - k + m, m)
        theirs = pl.ds(pl.multiple_of(source * share, share), share)
        remote(left_ref.at[theirs], left_ref.at[theirs], l2_send.at[k - 1], l2_recv.at[k - 1],
               (f, source)).wait_recv()

    left = left_ref[...]
    gpart[...] = dot(left, left, ((0,), (0,)))
    gshare = gpart.shape[0] // m
    gmine = pl.ds(pl.multiple_of(t * gshare, gshare), gshare)
    for k in range(1, n):
        d = lax.rem(f + k, n)
        remote(gpart.at[gmine], grecv.at[f], q_send.at[k - 1], q_recv.at[k - 1], (d, t)).start()
    grecv[f] = gpart[gmine, :]

    for j in range(wide // tile):
        col = slice(j * tile, (j + 1) * tile)
        spart[col, :] = dot(buf_ref[:, col], left, ((0,), (0,)))
    sshare = wide // n
    for k in range(1, n):
        d = lax.rem(f + k, n)
        remote(spart.at[pl.ds(pl.multiple_of(d * sshare, sshare), sshare)], srecv.at[k - 1],
               s_send.at[k - 1], s_recv.at[k - 1], (d, t)).start()

    for k in range(1, n):
        source = lax.rem(f - k + n, n)
        remote(gpart.at[gmine], grecv.at[source], q_send.at[k - 1], q_recv.at[k - 1],
               (source, t)).wait_recv()
    gram_ref[gmine, :] = jnp.sum(grecv[...], axis=0)
    for k in range(1, m):
        d = lax.rem(t + k, m)
        remote(gram_ref.at[gmine], gram_ref.at[gmine], q2_send.at[k - 1], q2_recv.at[k - 1],
               (f, d)).start()

    smine = pl.ds(pl.multiple_of(f * sshare, sshare), sshare)
    for k in range(1, n):
        remote(spart.at[smine], srecv.at[k - 1], s_send.at[k - 1], s_recv.at[k - 1],
               (f, t)).wait_recv()
    total = spart[smine, :]
    for k in range(1, n):
        total = total + srecv[k - 1]
    s_ref[smine, :] = total
    for k in range(1, n):
        d = lax.rem(f + k, n)
        remote(s_ref.at[smine], s_ref.at[smine], s2_send.at[k - 1], s2_recv.at[k - 1], (d, t)).start()

    for k in range(1, m):
        source = lax.rem(t - k + m, m)
        theirs = pl.ds(pl.multiple_of(source * gshare, gshare), gshare)
        remote(gram_ref.at[theirs], gram_ref.at[theirs], q2_send.at[k - 1], q2_recv.at[k - 1],
               (f, source)).wait_recv()
    for k in range(1, n):
        source = lax.rem(f - k + n, n)
        theirs = pl.ds(pl.multiple_of(source * sshare, sshare), sshare)
        remote(s_ref.at[theirs], s_ref.at[theirs], s2_send.at[k - 1], s2_recv.at[k - 1],
               (source, t)).wait_recv()

    for k in range(1, n):
        d = lax.rem(f + k, n)
        remote(gsend.at[d], ggath.at[f, t], gs_send.at[k - 1], gs_recv.at[k - 1], (d, t)).wait_send()
        remote(gpart.at[gmine], grecv.at[f], q_send.at[k - 1], q_recv.at[k - 1], (d, t)).wait_send()
        remote(spart.at[pl.ds(pl.multiple_of(d * sshare, sshare), sshare)], srecv.at[k - 1],
               s_send.at[k - 1], s_recv.at[k - 1], (d, t)).wait_send()
        remote(s_ref.at[smine], s_ref.at[smine], s2_send.at[k - 1], s2_recv.at[k - 1], (d, t)).wait_send()
    for k in range(1, m):
        d = lax.rem(t + k, m)
        remote(ggath.at[:, t], ggath.at[:, t], gt_send.at[k - 1], gt_recv.at[k - 1], (f, d)).wait_send()
        remote(lpart.at[pl.ds(pl.multiple_of(d * share, share), share)], lrecv.at[k - 1],
               l_send.at[k - 1], l_recv.at[k - 1], (f, d)).wait_send()
        remote(left_ref.at[mine], left_ref.at[mine], l2_send.at[k - 1], l2_recv.at[k - 1], (f, d)).wait_send()
        remote(gram_ref.at[gmine], gram_ref.at[gmine], q2_send.at[k - 1], q2_recv.at[k - 1],
               (f, d)).wait_send()
    for zz in range(nz):
        ax(2 * zz + x).wait_send()
    for k in range(nz):
        pl.when((z >= k) & (z < nz - 1))(lambda k=k: az(f - 2 * k, 0, k).wait_send())
        pl.when((z + k < nz) & (z > 0))(lambda k=k: az(f + 2 * k, 1, k).wait_send())


def split3(v):
    h = v.astype(BF16)
    r = v - h.astype(F32)
    mid = r.astype(BF16)
    return h.astype(F32), mid.astype(F32), r - mid.astype(F32)


def inverse_factor_kernel(gram_ref, inv_ref, work):
    rank = gram_ref.shape[0]
    work[:, :rank] = gram_ref[...]
    row = lax.broadcasted_iota(jnp.int32, (rank, rank), 0)
    col = lax.broadcasted_iota(jnp.int32, (rank, rank), 1)
    work[:, rank:] = jnp.where(row == col, 1.0, 0.0).astype(F32)
    sub = lax.broadcasted_iota(jnp.int32, (PANEL, 1), 0)
    lane = lax.broadcasted_iota(jnp.int32, (PANEL, rank), 1)

    def step(k, carry):
        start = pl.multiple_of(k * PANEL, PANEL)
        panel = work[pl.ds(start, PANEL), :]
        near = pltpu.roll(panel[:, :rank], lax.rem(rank - start, rank), 1)[:, :LANES]
        pivots = jnp.ones((PANEL, 1), F32)
        for j in range(PANEL):
            column = near[:, j:j + 1]
            pivot = column[j:j + 1, :]
            weight = jnp.where(sub > j, column / pivot, 0.0)
            pivots = jnp.where(sub == j, pivot, pivots)
            near = near - weight * near[j:j + 1, :]
            panel = panel - weight * panel[j:j + 1, :]
        panel = panel * lax.rsqrt(pivots)
        inv_ref[pl.ds(start, PANEL), :] = panel[:, rank:]
        outer = jnp.where(lane >= start + PANEL, panel[:, :rank], 0.0)
        h, mid, low = split3(outer)
        ph, pm, plow = split3(panel)
        lhs = jnp.concatenate([h, h, mid, h, mid, low], axis=0).astype(BF16)
        rhs = jnp.concatenate([ph, pm, ph, plow, pm, ph], axis=0).astype(BF16)
        work[...] = work[...] - lax.dot_general(
            lhs, rhs, (((0,), (0,)), ((), ())), preferred_element_type=F32)
        return carry

    lax.fori_loop(0, rank // PANEL, step, 0)


def factor_kernel(m, size, left_ref, s_ref, inv_ref, basis_ref, right_ref, factor_ref,
                  squares, send, recv):
    f = lax.axis_index("fsdp")
    t = lax.axis_index("tp")
    barrier = pltpu.get_barrier_semaphore()
    for k in range(1, m):
        pl.semaphore_signal(barrier, inc=1, device_id=(f, lax.rem(t + k, m)),
                            device_id_type=pl.DeviceIdType.MESH)
    inv = inv_ref[...]
    right = dot(s_ref[...], inv, ((1,), (1,)))
    right_ref[...] = right
    squares[t] = jnp.broadcast_to(jnp.sum(right * right, axis=0, keepdims=True), squares.shape[1:])
    pl.semaphore_wait(barrier, m - 1)
    copies = [
        remote(squares.at[t], squares.at[t], send.at[k - 1], recv.at[k - 1],
               (f, lax.rem(t + k, m)))
        for k in range(1, m)
    ]
    for copy in copies:
        copy.start()
    basis_ref[...] = dot(left_ref[...], inv, ((1,), (1,)))
    for k in range(1, m):
        source = lax.rem(t - k + m, m)
        remote(squares.at[source], squares.at[source], send.at[k - 1], recv.at[k - 1],
               (f, source)).wait_recv()
    factor_ref[...] = lax.rsqrt(jnp.sum(squares[...], axis=0) / size + 1e-06)
    for copy in copies:
        copy.wait_send()


def output_kernel(scale, buf_ref, basis_ref, right_ref, factor_ref, mom_ref, up_ref, hi, lo):
    @pl.when(pl.program_id(0) == 0)
    def _():
        r = right_ref[...]
        h = r.astype(BF16)
        hi[...] = h
        lo[...] = (r - h.astype(F32)).astype(BF16)

    basis = basis_ref[...]
    both = jnp.concatenate([basis * (momentum_decay - 1.0), basis * (factor_ref[0:1, :] * scale)], axis=0)
    bh = both.astype(BF16)
    bl = (both - bh.astype(F32)).astype(BF16)
    dims = (((1,), (1,)), ((), ()))
    out = lax.dot_general(bh, hi[...], dims, preferred_element_type=F32)
    out += lax.dot_general(bl, hi[...], dims, preferred_element_type=F32)
    out += lax.dot_general(bh, lo[...], dims, preferred_element_type=F32)
    tall = basis.shape[0]
    mom_ref[...] = buf_ref[...] + out[:tall]
    up_ref[...] = out[tall:]


def sds(*shape):
    return jax.ShapeDtypeStruct(shape, F32)


def kernels_on_device(n, m, activations, out_grad, momentum, right_prev):
    tok, wide = activations.shape
    rows = momentum.shape[0]
    rank = right_prev.shape[1]
    vm = pl.BlockSpec(memory_space=pltpu.VMEM)
    dma = pltpu.SemaphoreType.DMA
    full = rows * n
    nz = n // 2
    buffer, left, gram, s = pl.pallas_call(
        functools.partial(main_kernel, n, m),
        out_shape=(sds(rows, wide), sds(rows, rank), sds(rank, rank), sds(wide, rank)),
        in_specs=[vm] * 4,
        out_specs=(vm,) * 4,
        scratch_shapes=[
            pltpu.VMEM((n, tok, wide), F32),
            pltpu.VMEM((n, m, tok // m, rows), F32),
            pltpu.VMEM((n, tok // m, rows), F32),
            pltpu.VMEM((rows, n * tok), BF16),
            pltpu.VMEM((rows, rank), F32),
            pltpu.VMEM((m - 1, rows // m, rank), F32),
            pltpu.VMEM((rank, rank), F32),
            pltpu.VMEM((n, rank // m, rank), F32),
            pltpu.VMEM((wide, rank), F32),
            pltpu.VMEM((n - 1, wide // n, rank), F32),
            dma((2, nz)), dma((nz,)), dma((nz,)), dma((nz,)),
            dma((n - 1,)), dma((n - 1,)), dma((m - 1,)), dma((m - 1,)),
            dma((m - 1,)), dma((m - 1,)), dma((m - 1,)), dma((m - 1,)),
            dma((n - 1,)), dma((n - 1,)), dma((m - 1,)), dma((m - 1,)),
            dma((n - 1,)), dma((n - 1,)), dma((n - 1,)), dma((n - 1,)),
        ],
        compiler_params=pltpu.CompilerParams(
            collective_id=0, has_side_effects=True, vmem_limit_bytes=VMEM_LIMIT),
    )(activations, out_grad, momentum, right_prev)
    inverse = pl.pallas_call(
        inverse_factor_kernel,
        out_shape=sds(rank, rank),
        in_specs=[vm],
        out_specs=vm,
        scratch_shapes=[pltpu.VMEM((rank, 2 * rank), F32)],
    )(gram)
    basis, right, factor = pl.pallas_call(
        functools.partial(factor_kernel, m, full),
        out_shape=(sds(rows, rank), sds(wide, rank), sds(8, rank)),
        in_specs=[vm] * 3,
        out_specs=(vm,) * 3,
        scratch_shapes=[pltpu.VMEM((m, 8, rank), F32), dma((m - 1,)), dma((m - 1,))],
        compiler_params=pltpu.CompilerParams(
            collective_id=1, has_side_effects=True, vmem_limit_bytes=VMEM_LIMIT),
    )(left, s, inverse)
    tall = LANES
    size = wide * m
    new_momentum, update = pl.pallas_call(
        functools.partial(output_kernel, math.sqrt(size / rank)),
        grid=(rows // tall,),
        out_shape=(sds(rows, wide), sds(rows, wide)),
        in_specs=[
            pl.BlockSpec((tall, wide), lambda i: (i, 0)),
            pl.BlockSpec((tall, rank), lambda i: (i, 0)),
            pl.BlockSpec((wide, rank), lambda i: (0, 0)),
            pl.BlockSpec((8, rank), lambda i: (0, 0)),
        ],
        out_specs=(
            pl.BlockSpec((tall, wide), lambda i: (i, 0)),
            pl.BlockSpec((tall, wide), lambda i: (i, 0)),
        ),
        scratch_shapes=[pltpu.VMEM((wide, rank), BF16)] * 2,
        compiler_params=pltpu.CompilerParams(vmem_limit_bytes=VMEM_LIMIT),
    )(buffer, basis, right, factor)
    own = rank // n
    first = lax.axis_index("fsdp") * own
    right_owned = lax.dynamic_slice_in_dim(right, first, own, 1) * lax.dynamic_slice_in_dim(
        factor[0:1], first, own, 1)
    return new_momentum, update, right_owned


def plain_on_device(activations, out_grad, momentum, right_prev):
    size = momentum.shape[1] * lax.axis_size("tp")
    rank = right_prev.shape[1]
    grad = lax.psum_scatter(
        lax.dot_general(out_grad, activations, (((0,), (0,)), ((), ())), preferred_element_type=F32),
        "fsdp", scatter_dimension=0, tiled=True)
    buffer = momentum + grad
    left = lax.psum(dot(buffer, right_prev), "tp")
    gram = lax.psum(dot(left.T, left), "fsdp")
    lower = jnp.linalg.cholesky(gram)
    basis = lax.linalg.triangular_solve(lower, left, left_side=False, lower=True, transpose_a=True)
    right = lax.psum(dot(buffer.T, basis), "fsdp")
    squares = lax.psum(jnp.sum(right * right, axis=0), "tp")
    factor = lax.rsqrt(squares / size + 1e-06)
    right_next = right * factor[None, :]
    new_momentum = buffer - (1.0 - momentum_decay) * dot(basis, right.T)
    update = math.sqrt(size / rank) * dot(basis, right_next.T)
    own = rank // lax.axis_size("fsdp")
    right_owned = lax.dynamic_slice_in_dim(right_next, lax.axis_index("fsdp") * own, own, 1)
    return new_momentum, update, right_owned


def solution(mesh):
    n, m = mesh.shape["fsdp"], mesh.shape["tp"]

    def on_device(activations, out_grad, momentum, right_prev):
        tok, wide = activations.shape
        rows = momentum.shape[0]
        if rows % LANES == 0 and wide % (2 * LANES) == 0 and 4 * n * tok * (wide + rows) <= VMEM_LIMIT // 4:
            return kernels_on_device(n, m, activations, out_grad, momentum, right_prev)
        return plain_on_device(activations, out_grad, momentum, right_prev)

    return jax.shard_map(
        on_device,
        mesh=mesh,
        in_specs=(P("fsdp", "tp"), P("fsdp", None), P("fsdp", "tp"), P("tp", None)),
        out_specs=(P("fsdp", "tp"), P("fsdp", "tp"), P("tp", "fsdp")),
        check_vma=False,
    )
```

time: 752 us -> 224 us (0.30); the launches traced: 742 us -> 224 us
  waiting for transfers between devices: 605 us -> 0 us
  Pallas kernels: 0 us -> 221 us
  other arithmetic: 59.7 us -> 0.24 us
  matrix products: 44.6 us -> 0 us
  between operations: 15.6 us -> 0.67 us
  local copies, waits for them, and re-layouts: 11.1 us -> 1.65 us
    reduce_scatter x1 -> x0, waiting for transfers between devices: 418 us -> none  [on_device(): lax.psum_scatter(token_product(out_grad, activations), 'fsdp', scatter_di...]
    pallas_call x0 -> x4, Pallas kernels: none -> 221 us  [the longest x1 173 us: kernels_on_device(): pl.pallas_call(functools.partial(main_kernel, n, m), out_shape=(sds(rows,...]
    psum x3 -> x0, waiting for transfers between devices: 187 us -> none  [the longest x1 84.6 us: on_device(): right = lax.psum(partial_right, 'fsdp')]
    another operation x9 -> x0, other arithmetic: 53.7 us -> none  [the longest x6 34 us: on_device(): lower = jnp.linalg.cholesky(gram)]
    dot_general x6 -> x0, matrix products: 42.5 us -> none  [the longest x1 11.5 us: token_product(): lax.dot_general(out_grad, columns_in, (((0,), (0,)), ((), ())), preferred...]
  transfers between devices with their start and end apart: 4 -> 0, of which waited for: 4 -> 0; matrix products, arithmetic and copies ran while one was open for 0% -> 0% of each run, Pallas kernels for 0% -> 0%
where the time goes in v1:
time: 224 us
  Pallas kernels  221 us (99%)
    pallas_call x1, Pallas kernels, kernels_on_device(): pl.pallas_call(functools.partial(main_kernel, n, m), out_shape=(sds(rows,...  173 us
    pallas_call x1, Pallas kernels, kernels_on_device(): pl.pallas_call(inverse_factor_kernel, out_shape=sds(rank, rank), in_specs...  32.1 us
    pallas_call x1, Pallas kernels, kernels_on_device(): pl.pallas_call(functools.partial(output_kernel, math.sqrt(size / rank)),...  8.22 us
    pallas_call x1, Pallas kernels, kernels_on_device(): pl.pallas_call(functools.partial(factor_kernel, m, full), out_shape=(sds(...  7.94 us

profile of v1, /device:TPU:27, one launch (start us, length us, event | category | flops | bytes accessed | tf_op | source)
XLA Modules:
  0.0 223.8 jit_solution(888745727867896798)
XLA Ops:
  0.6 173.0 %shard_map.67 = (f32[640,1280]{1,0:T(8,128)}, f32[640,256]{1,0:T(8,128)}, f32[256,256]{1,0:T(8,128)}, f32[1280,256]{1,0:T(8,128)}) custom-call(bf16[128,1280]{1,0:T(8,128)(2,1)} %a_ref.1, bf16[128,5120]{1,0:T(8,128)(2,1)} %g_ref.1, f32[640,1280]{1,0:T(8,128)} %mom_ref.1, f32[1280,256]{1,0:T(8,128)} %p_ref.1), custom_call_target="tpu_custom_call" | custom-call | tf_op jit(solution)/shard_map/pallas_call | solution.py:327
  173.7 32.1 %shard_map.68.inv_ref = f32[256,256]{1,0:T(8,128)} custom-call(f32[256,256]{1,0:T(8,128)} %get-tuple-element.15.gram_ref), custom_call_target="tpu_custom_call" | custom-call | tf_op jit(solution)/shard_map/pallas_call | solution.py:352
  205.7 7.9 %shard_map.69 = (f32[640,256]{1,0:T(8,128)}, f32[1280,256]{1,0:T(8,128)}, f32[8,256]{1,0:T(8,128)}) custom-call(f32[640,256]{1,0:T(8,128)} %get-tuple-element.13.left_ref, f32[1280,256]{1,0:T(8,128)} %get-tuple-element.14.s_ref, f32[256,256]{1,0:T(8,128)} %shard_map.68.inv_ref), custom_call_target="tpu_custom_call" | custom-call | tf_op jit(solution)/shard_map/pallas_call | solution.py:359
  213.7 0.0 copy-start
  213.7 8.2 %shard_map.70 = (f32[640,1280]{1,0:T(8,128)}, f32[640,1280]{1,0:T(8,128)}) custom-call(f32[640,1280]{1,0:T(8,128)} %get-tuple-element.12.buf_ref, f32[640,256]{1,0:T(8,128)} %get-tuple-element.16.basis_ref, f32[1280,256]{1,0:T(8,128)} %get-tuple-element.17.right_ref, f32[8,256]{1,0:T(8,128)} %get-tuple-element.18.factor_ref), custom_call_target="tpu_custom_call" | custom-call | tf_op jit(solution)/shard_map/pallas_call | solution.py:370
  221.9 0.7 slice.3
  222.6 0.1 dynamic-slice_bitcast_fusion
  222.7 0.0 copy-done
  222.7 0.2 dynamic-slice_multiply_fusion
  222.9 0.9 copy.7
Async XLA Ops:
  213.7 9.0 %copy-start = (f32[1280,256]{1,0:T(8,128)S(1)}, f32[1280,256]{1,0:T(8,128)}, u32[]{:S(2)}) copy-start(f32[1280,256]{1,0:T(8,128)} %get-tuple-element.17.right_ref) | copy-start | bytes 3932164

commit v2 on v1

--- a/solution.py
+++ b/solution.py
@@ -41,7 +41,8 @@
 
 
 def main_kernel(n, m, a_ref, g_ref, mom_ref, p_ref,
-                buf_ref, left_ref, gram_ref, s_ref,
+                buf_ref, basis_ref, right_ref, factor_ref,
+                left_ref, gram_ref, s_ref, inv_ref, work, squares, c_send, c_recv,
                 agath, ggath, gsend, gt, lpart, lrecv, gpart, grecv, spart, srecv,
                 az_send, az_recv, ax_send, ax_recv, gs_send, gs_recv, gt_send, gt_recv,
                 l_send, l_recv, l2_send, l2_recv, q_send, q_recv, q2_send, q2_recv,
@@ -174,28 +175,46 @@
         remote(gram_ref.at[gmine], gram_ref.at[gmine], q2_send.at[k - 1], q2_recv.at[k - 1],
                (f, d)).start()
 
-    smine = pl.ds(pl.multiple_of(f * sshare, sshare), sshare)
-    for k in range(1, n):
-        remote(spart.at[smine], srecv.at[k - 1], s_send.at[k - 1], s_recv.at[k - 1],
-               (f, t)).wait_recv()
-    total = spart[smine, :]
-    for k in range(1, n):
-        total = total + srecv[k - 1]
-    s_ref[smine, :] = total
-    for k in range(1, n):
-        d = lax.rem(f + k, n)
-        remote(s_ref.at[smine], s_ref.at[smine], s2_send.at[k - 1], s2_recv.at[k - 1], (d, t)).start()
-
     for k in range(1, m):
         source = lax.rem(t - k + m, m)
         theirs = pl.ds(pl.multiple_of(source * gshare, gshare), gshare)
         remote(gram_ref.at[theirs], gram_ref.at[theirs], q2_send.at[k - 1], q2_recv.at[k - 1],
                (f, source)).wait_recv()
+    inv_ref[...] = jnp.zeros_like(inv_ref)
+    inverse_begin(gram_ref, work)
+    inverse_rows(work, inv_ref, 0, gram_ref.shape[0] // 2)
+    smine = pl.ds(pl.multiple_of(f * sshare, sshare), sshare)
+    for k in range(1, n):
+        remote(spart.at[smine], srecv.at[k - 1], s_send.at[k - 1], s_recv.at[k - 1],
+               (f, t)).wait_recv()
+    total = spart[smine, :]
+    for k in range(1, n):
+        total = total + srecv[k - 1]
+    s_ref[smine, :] = total
+    for k in range(1, n):
+        d = lax.rem(f + k, n)
+        remote(s_ref.at[smine], s_ref.at[smine], s2_send.at[k - 1], s2_recv.at[k - 1], (d, t)).start()
+
+    inverse_rows(work, inv_ref, gram_ref.shape[0] // 2, gram_ref.shape[0])
+    inv = inv_ref[...]
     for k in range(1, n):
         source = lax.rem(f - k + n, n)
         theirs = pl.ds(pl.multiple_of(source * sshare, sshare), sshare)
         remote(s_ref.at[theirs], s_ref.at[theirs], s2_send.at[k - 1], s2_recv.at[k - 1],
                (source, t)).wait_recv()
+
+    right = dot(s_ref[...], inv, ((1,), (1,)))
+    right_ref[...] = right
+    squares[t] = jnp.broadcast_to(jnp.sum(right * right, axis=0, keepdims=True), squares.shape[1:])
+    for k in range(1, m):
+        remote(squares.at[t], squares.at[t], c_send.at[k - 1], c_recv.at[k - 1],
+               (f, lax.rem(t + k, m))).start()
+    basis_ref[...] = dot(left_ref[...], inv, ((1,), (1,)))
+    for k in range(1, m):
+        source = lax.rem(t - k + m, m)
+        remote(squares.at[source], squares.at[source], c_send.at[k - 1], c_recv.at[k - 1],
+               (f, source)).wait_recv()
+    factor_ref[...] = lax.rsqrt(jnp.sum(squares[...], axis=0) / (rows * n) + 1e-06)
 
     for k in range(1, n):
         d = lax.rem(f + k, n)
@@ -212,6 +231,7 @@
         remote(left_ref.at[mine], left_ref.at[mine], l2_send.at[k - 1], l2_recv.at[k - 1], (f, d)).wait_send()
         remote(gram_ref.at[gmine], gram_ref.at[gmine], q2_send.at[k - 1], q2_recv.at[k - 1],
                (f, d)).wait_send()
+        remote(squares.at[t], squares.at[t], c_send.at[k - 1], c_recv.at[k - 1], (f, d)).wait_send()
     for zz in range(nz):
         ax(2 * zz + x).wait_send()
     for k in range(nz):
@@ -226,69 +246,47 @@
     return h.astype(F32), mid.astype(F32), r - mid.astype(F32)
 
 
-def inverse_factor_kernel(gram_ref, inv_ref, work):
+def inverse_begin(gram_ref, work):
     rank = gram_ref.shape[0]
     work[:, :rank] = gram_ref[...]
     row = lax.broadcasted_iota(jnp.int32, (rank, rank), 0)
     col = lax.broadcasted_iota(jnp.int32, (rank, rank), 1)
     work[:, rank:] = jnp.where(row == col, 1.0, 0.0).astype(F32)
+
+
+def inverse_rows(work, inv_ref, first, last):
+    rank = work.shape[0]
+    some = LANES // 2
     sub = lax.broadcasted_iota(jnp.int32, (PANEL, 1), 0)
-    lane = lax.broadcasted_iota(jnp.int32, (PANEL, rank), 1)
-
-    def step(k, carry):
-        start = pl.multiple_of(k * PANEL, PANEL)
-        panel = work[pl.ds(start, PANEL), :]
-        near = pltpu.roll(panel[:, :rank], lax.rem(rank - start, rank), 1)[:, :LANES]
-        pivots = jnp.ones((PANEL, 1), F32)
-        for j in range(PANEL):
-            column = near[:, j:j + 1]
-            pivot = column[j:j + 1, :]
-            weight = jnp.where(sub > j, column / pivot, 0.0)
-            pivots = jnp.where(sub == j, pivot, pivots)
-            near = near - weight * near[j:j + 1, :]
-            panel = panel - weight * panel[j:j + 1, :]
-        panel = panel * lax.rsqrt(pivots)
-        inv_ref[pl.ds(start, PANEL), :] = panel[:, rank:]
-        outer = jnp.where(lane >= start + PANEL, panel[:, :rank], 0.0)
-        h, mid, low = split3(outer)
-        ph, pm, plow = split3(panel)
-        lhs = jnp.concatenate([h, h, mid, h, mid, low], axis=0).astype(BF16)
-        rhs = jnp.concatenate([ph, pm, ph, plow, pm, ph], axis=0).astype(BF16)
-        work[...] = work[...] - lax.dot_general(
-            lhs, rhs, (((0,), (0,)), ((), ())), preferred_element_type=F32)
-        return carry
-
-    lax.fori_loop(0, rank // PANEL, step, 0)
-
-
-def factor_kernel(m, size, left_ref, s_ref, inv_ref, basis_ref, right_ref, factor_ref,
-                  squares, send, recv):
-    f = lax.axis_index("fsdp")
-    t = lax.axis_index("tp")
-    barrier = pltpu.get_barrier_semaphore()
-    for k in range(1, m):
-        pl.semaphore_signal(barrier, inc=1, device_id=(f, lax.rem(t + k, m)),
-                            device_id_type=pl.DeviceIdType.MESH)
-    inv = inv_ref[...]
-    right = dot(s_ref[...], inv, ((1,), (1,)))
-    right_ref[...] = right
-    squares[t] = jnp.broadcast_to(jnp.sum(right * right, axis=0, keepdims=True), squares.shape[1:])
-    pl.semaphore_wait(barrier, m - 1)
-    copies = [
-        remote(squares.at[t], squares.at[t], send.at[k - 1], recv.at[k - 1],
-               (f, lax.rem(t + k, m)))
-        for k in range(1, m)
-    ]
-    for copy in copies:
-        copy.start()
-    basis_ref[...] = dot(left_ref[...], inv, ((1,), (1,)))
-    for k in range(1, m):
-        source = lax.rem(t - k + m, m)
-        remote(squares.at[source], squares.at[source], send.at[k - 1], recv.at[k - 1],
-               (f, source)).wait_recv()
-    factor_ref[...] = lax.rsqrt(jnp.sum(squares[...], axis=0) / size + 1e-06)
-    for copy in copies:
-        copy.wait_send()
+    for top in range(first, last, some):
+        base = top // LANES * LANES
+        end = rank + base + LANES
+        lane = lax.broadcasted_iota(jnp.int32, (PANEL, rank - base), 1) + base
+
+        def step(k, carry):
+            start = pl.multiple_of(top + k * PANEL, PANEL)
+            panel = work[pl.ds(start, PANEL), base:end]
+            near = pltpu.roll(panel[:, :LANES], lax.rem(base + LANES - start, LANES), 1)
+            pivots = jnp.ones((PANEL, 1), F32)
+            for j in range(PANEL):
+                column = near[:, j:j + 1]
+                pivot = column[j:j + 1, :]
+                weight = jnp.where(sub > j, column / pivot, 0.0)
+                pivots = jnp.where(sub == j, pivot, pivots)
+                near = near - weight * near[j:j + 1, :]
+                panel = panel - weight * panel[j:j + 1, :]
+            panel = panel * lax.rsqrt(pivots)
+            inv_ref[pl.ds(start, PANEL), :base + LANES] = panel[:, rank - base:]
+            outer = jnp.where(lane >= start + PANEL, panel[:, :rank - base], 0.0)[:, top - base:]
+            h, mid, low = split3(outer)
+            ph, pm, plow = split3(panel)
+            lhs = jnp.concatenate([h, h, mid, h, mid, low], axis=0).astype(BF16)
+            rhs = jnp.concatenate([ph, pm, ph, plow, pm, ph], axis=0).astype(BF16)
+            work[top:, base:end] = work[top:, base:end] - lax.dot_general(
+                lhs, rhs, (((0,), (0,)), ((), ())), preferred_element_type=F32)
+            return carry
+
+        lax.fori_loop(0, some // PANEL, step, 0)
 
 
 def output_kernel(scale, buf_ref, basis_ref, right_ref, factor_ref, mom_ref, up_ref, hi, lo):
@@ -322,14 +320,20 @@
     rank = right_prev.shape[1]
     vm = pl.BlockSpec(memory_space=pltpu.VMEM)
     dma = pltpu.SemaphoreType.DMA
-    full = rows * n
     nz = n // 2
-    buffer, left, gram, s = pl.pallas_call(
+    buffer, basis, right, factor = pl.pallas_call(
         functools.partial(main_kernel, n, m),
-        out_shape=(sds(rows, wide), sds(rows, rank), sds(rank, rank), sds(wide, rank)),
+        out_shape=(sds(rows, wide), sds(rows, rank), sds(wide, rank), sds(8, rank)),
         in_specs=[vm] * 4,
         out_specs=(vm,) * 4,
         scratch_shapes=[
+            pltpu.VMEM((rows, rank), F32),
+            pltpu.VMEM((rank, rank), F32),
+            pltpu.VMEM((wide, rank), F32),
+            pltpu.VMEM((rank, rank), F32),
+            pltpu.VMEM((rank, 2 * rank), F32),
+            pltpu.VMEM((m, 8, rank), F32),
+            dma((m - 1,)), dma((m - 1,)),
             pltpu.VMEM((n, tok, wide), F32),
             pltpu.VMEM((n, m, tok // m, rows), F32),
             pltpu.VMEM((n, tok // m, rows), F32),
@@ -349,22 +353,6 @@
         compiler_params=pltpu.CompilerParams(
             collective_id=0, has_side_effects=True, vmem_limit_bytes=VMEM_LIMIT),
     )(activations, out_grad, momentum, right_prev)
-    inverse = pl.pallas_call(
-        inverse_factor_kernel,
-        out_shape=sds(rank, rank),
-        in_specs=[vm],
-        out_specs=vm,
-        scratch_shapes=[pltpu.VMEM((rank, 2 * rank), F32)],
-    )(gram)
-    basis, right, factor = pl.pallas_call(
-        functools.partial(factor_kernel, m, full),
-        out_shape=(sds(rows, rank), sds(wide, rank), sds(8, rank)),
-        in_specs=[vm] * 3,
-        out_specs=(vm,) * 3,
-        scratch_shapes=[pltpu.VMEM((m, 8, rank), F32), dma((m - 1,)), dma((m - 1,))],
-        compiler_params=pltpu.CompilerParams(
-            collective_id=1, has_side_effects=True, vmem_limit_bytes=VMEM_LIMIT),
-    )(left, s, inverse)
     tall = LANES
     size = wide * m
     new_momentum, update = pl.pallas_call(

time: 224 us -> 197 us (0.88)
  Pallas kernels: 221 us -> 194 us
    pallas_call x2 -> x0, Pallas kernels: 40 us -> none  [the longest x1 32.1 us: kernels_on_device(): pl.pallas_call(inverse_factor_kernel, out_shape=sds(rank, rank), in_specs...]
    pallas_call x1, Pallas kernels: 173 us -> 186 us  [kernels_on_device(): pl.pallas_call(functools.partial(main_kernel, n, m), out_shape=(sds(rows,...]
where the time goes in v2:
time: 197 us; the launch traced here: 196 us
  Pallas kernels  194 us (98%)
    pallas_call x1, Pallas kernels, kernels_on_device(): pl.pallas_call(functools.partial(main_kernel, n, m), out_shape=(sds(rows,...  186 us
    pallas_call x1, Pallas kernels, kernels_on_device(): pl.pallas_call(functools.partial(output_kernel, math.sqrt(size / rank)),...  8.23 us

profile of v2, /device:TPU:27, one launch (start us, length us, event | category | flops | bytes accessed | tf_op | source)
XLA Modules:
  0.0 196.3 jit_solution(16807451407766345064)
XLA Ops:
  0.6 185.6 %shard_map.67 = (f32[640,1280]{1,0:T(8,128)}, f32[640,256]{1,0:T(8,128)}, f32[1280,256]{1,0:T(8,128)}, f32[8,256]{1,0:T(8,128)}) custom-call(bf16[128,1280]{1,0:T(8,128)(2,1)} %a_ref.1, bf16[128,5120]{1,0:T(8,128)(2,1)} %g_ref.1, f32[640,1280]{1,0:T(8,128)} %mom_ref.1, f32[1280,256]{1,0:T(8,128)} %p_ref.1), custom_call_target="tpu_custom_call" | custom-call | tf_op jit(solution)/shard_map/pallas_call | solution.py:324
  186.2 0.0 copy-start
  186.2 8.2 %shard_map.68 = (f32[640,1280]{1,0:T(8,128)}, f32[640,1280]{1,0:T(8,128)}) custom-call(f32[640,1280]{1,0:T(8,128)} %get-tuple-element.9.buf_ref, f32[640,256]{1,0:T(8,128)} %get-tuple-element.10.basis_ref, f32[1280,256]{1,0:T(8,128)} %get-tuple-element.11.right_ref, f32[8,256]{1,0:T(8,128)} %get-tuple-element.12.factor_ref), custom_call_target="tpu_custom_call" | custom-call | tf_op jit(solution)/shard_map/pallas_call | solution.py:358
  194.4 0.7 slice.3
  195.1 0.1 dynamic-slice_bitcast_fusion
  195.2 0.0 copy-done
  195.2 0.2 dynamic-slice_multiply_fusion
  195.4 0.9 copy.7
Async XLA Ops:
  186.2 9.0 %copy-start = (f32[1280,256]{1,0:T(8,128)S(1)}, f32[1280,256]{1,0:T(8,128)}, u32[]{:S(2)}) copy-start(f32[1280,256]{1,0:T(8,128)} %get-tuple-element.11.right_ref) | copy-start | bytes 3932164

commit v3 on v2

--- a/solution.py
+++ b/solution.py
@@ -13,6 +13,7 @@
 BF16 = jnp.bfloat16
 LANES = 128
 PANEL = 8
+CHUNKS = 4
 VMEM_LIMIT = 56 * 1024 * 1024
 
 momentum_decay = 0.95
@@ -40,9 +41,9 @@
     pl.semaphore_wait(barrier, n + m - 2)
 
 
-def main_kernel(n, m, a_ref, g_ref, mom_ref, p_ref,
-                buf_ref, basis_ref, right_ref, factor_ref,
-                left_ref, gram_ref, s_ref, inv_ref, work, squares, c_send, c_recv,
+def main_kernel(n, m, a_ref, g_ref, mom_ref, p_hbm,
+                buf_out, basis_ref, right_ref, factor_ref,
+                buf_ref, p_ref, own_sem, left_ref, gram_ref, s_ref, inv_ref, work, squares, c_send, c_recv,
                 agath, ggath, gsend, gt, lpart, lrecv, gpart, grecv, spart, srecv,
                 az_send, az_recv, ax_send, ax_recv, gs_send, gs_recv, gt_send, gt_recv,
                 l_send, l_recv, l2_send, l2_recv, q_send, q_recv, q2_send, q2_recv,
@@ -55,7 +56,12 @@
     tok, wide = a_ref.shape
     quarter = tok // m
     rows = mom_ref.shape[0]
-    agath[f] = a_ref[...].astype(F32)
+    load_momentum = pltpu.make_async_copy(mom_ref, buf_ref, own_sem.at[0])
+    load_right = pltpu.make_async_copy(p_hbm, p_ref, own_sem.at[1])
+    store_buffer = pltpu.make_async_copy(buf_ref, buf_out, own_sem.at[2])
+    load_momentum.start()
+    load_right.start()
+    agath[f] = a_ref[...].astype(F32).reshape(agath.shape[1:])
     for d in range(n):
         gsend[d] = g_ref[pl.ds(pl.multiple_of(t * quarter, quarter), quarter),
                          d * rows:(d + 1) * rows].astype(F32)
@@ -66,33 +72,35 @@
         d = lax.rem(f + k, n)
         remote(gsend.at[d], ggath.at[f, t], gs_send.at[k - 1], gs_recv.at[k - 1], (d, t)).start()
 
-    def az(slot, way, k):
+    def az(slot, c, way, k):
         target = (z + 1) * 2 + x if way == 0 else (z - 1) * 2 + x
-        sem = slot // 2
-        return remote(agath.at[slot], agath.at[slot], az_send.at[way, k], az_recv.at[sem], (target, t))
-
-    def ax(slot):
-        return remote(agath.at[slot], agath.at[slot], ax_send.at[slot // 2], ax_recv.at[slot // 2],
-                      (xpeer, t))
-
-    pl.when(z < nz - 1)(lambda: az(f, 0, 0).start())
-    pl.when(z > 0)(lambda: az(f, 1, 0).start())
-    ax(f).start()
+        return remote(agath.at[slot, c], agath.at[slot, c], az_send.at[way, k, c],
+                      az_recv.at[slot // 2, c], (target, t))
+
+    def ax(slot, c):
+        return remote(agath.at[slot, c], agath.at[slot, c], ax_send.at[slot // 2, c],
+                      ax_recv.at[slot // 2, c], (xpeer, t))
+
+    for c in range(CHUNKS):
+        pl.when(z < nz - 1)(lambda c=c: az(f, c, 0, 0).start())
+        pl.when(z > 0)(lambda c=c: az(f, c, 1, 0).start())
+        ax(f, c).start()
 
     def gather_step(k):
-        @pl.when(z >= k)
-        def _():
-            slot = f - 2 * k
-            az(slot, 0, k).wait_recv()
-            pl.when(z < nz - 1)(lambda: az(slot, 0, k).start())
-            ax(slot).start()
-
-        @pl.when(z + k < nz)
-        def _():
-            slot = f + 2 * k
-            az(slot, 1, k).wait_recv()
-            pl.when(z > 0)(lambda: az(slot, 1, k).start())
-            ax(slot).start()
+        for c in range(CHUNKS):
+            @pl.when(z >= k)
+            def _():
+                slot = f - 2 * k
+                az(slot, c, 0, k).wait_recv()
+                pl.when(z < nz - 1)(lambda: az(slot, c, 0, k).start())
+                ax(slot, c).start()
+
+            @pl.when(z + k < nz)
+            def _():
+                slot = f + 2 * k
+                az(slot, c, 1, k).wait_recv()
+                pl.when(z > 0)(lambda: az(slot, c, 1, k).start())
+                ax(slot, c).start()
 
     def gs_wait():
         for k in range(1, n):
@@ -113,18 +121,22 @@
                (f, source)).wait_recv()
     gt[...] = ggath[...].reshape(n * tok, rows).astype(BF16).T
     for zz in range(nz):
-        slot = 2 * zz + (1 - x)
-        remote(agath.at[slot], agath.at[slot], ax_send.at[zz], ax_recv.at[zz], (xpeer, t)).wait_recv()
-
+        for c in range(CHUNKS):
+            ax(2 * zz + (1 - x), c).wait_recv()
+
+    load_momentum.wait()
+    load_right.wait()
     tile = 2 * LANES
     for j in range(wide // tile):
         col = slice(j * tile, (j + 1) * tile)
-        part = agath[:, :, col].reshape(n * tok, tile).astype(BF16)
+        part = agath[:, :, :, col].reshape(n * tok, tile).astype(BF16)
         grad = jnp.dot(gt[...], part, preferred_element_type=F32)
-        b = mom_ref[:, col] + grad
+        b = buf_ref[:, col] + grad
         buf_ref[:, col] = b
         term = dot(b, p_ref[col, :])
         lpart[...] = term if j == 0 else lpart[...] + term
+
+    store_buffer.start()
 
     share = rows // m
     for k in range(1, m):
@@ -191,18 +203,33 @@
     for k in range(1, n):
         total = total + srecv[k - 1]
     s_ref[smine, :] = total
-    for k in range(1, n):
-        d = lax.rem(f + k, n)
-        remote(s_ref.at[smine], s_ref.at[smine], s2_send.at[k - 1], s2_recv.at[k - 1], (d, t)).start()
-
-    inverse_rows(work, inv_ref, gram_ref.shape[0] // 2, gram_ref.shape[0])
+
+    def s_rows(owner):
+        return s_ref.at[pl.ds(pl.multiple_of(owner * sshare, sshare), sshare)]
+
+    def sz(owner, k):
+        return remote(s_rows(owner), s_rows(owner), s2_send.at[k - 1], s2_recv.at[k - 1],
+                      (lax.rem(z + k, nz) * 2 + x, t))
+
+    def sx(owner, k):
+        return remote(s_rows(owner), s_rows(owner), s2_send.at[nz - 1 + k], s2_recv.at[nz - 1 + k],
+                      (xpeer, t))
+
+    def owner_at(k, side):
+        return lax.rem(z - k + nz, nz) * 2 + side
+
+    for k in range(1, nz):
+        sz(f, k).start()
+    sx(f, 0).start()
+    inverse_rows(work, inv_ref, gram_ref.shape[0] // 2, gram_ref.shape[0] * 3 // 4)
+    for k in range(1, nz):
+        sz(owner_at(k, x), k).wait_recv()
+        sx(owner_at(k, x), k).start()
+
+    inverse_rows(work, inv_ref, gram_ref.shape[0] * 3 // 4, gram_ref.shape[0])
     inv = inv_ref[...]
-    for k in range(1, n):
-        source = lax.rem(f - k + n, n)
-        theirs = pl.ds(pl.multiple_of(source * sshare, sshare), sshare)
-        remote(s_ref.at[theirs], s_ref.at[theirs], s2_send.at[k - 1], s2_recv.at[k - 1],
-               (source, t)).wait_recv()
-
+    for k in range(nz):
+        sx(owner_at(k, 1 - x), k).wait_recv()
     right = dot(s_ref[...], inv, ((1,), (1,)))
     right_ref[...] = right
     squares[t] = jnp.broadcast_to(jnp.sum(right * right, axis=0, keepdims=True), squares.shape[1:])
@@ -216,13 +243,13 @@
                (f, source)).wait_recv()
     factor_ref[...] = lax.rsqrt(jnp.sum(squares[...], axis=0) / (rows * n) + 1e-06)
 
+    store_buffer.wait()
     for k in range(1, n):
         d = lax.rem(f + k, n)
         remote(gsend.at[d], ggath.at[f, t], gs_send.at[k - 1], gs_recv.at[k - 1], (d, t)).wait_send()
         remote(gpart.at[gmine], grecv.at[f], q_send.at[k - 1], q_recv.at[k - 1], (d, t)).wait_send()
         remote(spart.at[pl.ds(pl.multiple_of(d * sshare, sshare), sshare)], srecv.at[k - 1],
                s_send.at[k - 1], s_recv.at[k - 1], (d, t)).wait_send()
-        remote(s_ref.at[smine], s_ref.at[smine], s2_send.at[k - 1], s2_recv.at[k - 1], (d, t)).wait_send()
     for k in range(1, m):
         d = lax.rem(t + k, m)
         remote(ggath.at[:, t], ggath.at[:, t], gt_send.at[k - 1], gt_recv.at[k - 1], (f, d)).wait_send()
@@ -232,11 +259,17 @@
         remote(gram_ref.at[gmine], gram_ref.at[gmine], q2_send.at[k - 1], q2_recv.at[k - 1],
                (f, d)).wait_send()
         remote(squares.at[t], squares.at[t], c_send.at[k - 1], c_recv.at[k - 1], (f, d)).wait_send()
+    for k in range(nz):
+        if k:
+            sz(f, k).wait_send()
+        sx(owner_at(k, x), k).wait_send()
     for zz in range(nz):
-        ax(2 * zz + x).wait_send()
+        for c in range(CHUNKS):
+            ax(2 * zz + x, c).wait_send()
     for k in range(nz):
-        pl.when((z >= k) & (z < nz - 1))(lambda k=k: az(f - 2 * k, 0, k).wait_send())
-        pl.when((z + k < nz) & (z > 0))(lambda k=k: az(f + 2 * k, 1, k).wait_send())
+        for c in range(CHUNKS):
+            pl.when((z >= k) & (z < nz - 1))(lambda k=k, c=c: az(f - 2 * k, c, 0, k).wait_send())
+            pl.when((z + k < nz) & (z > 0))(lambda k=k, c=c: az(f + 2 * k, c, 1, k).wait_send())
 
 
 def split3(v):
@@ -319,14 +352,18 @@
     rows = momentum.shape[0]
     rank = right_prev.shape[1]
     vm = pl.BlockSpec(memory_space=pltpu.VMEM)
+    hbm = pl.BlockSpec(memory_space=pl.ANY)
     dma = pltpu.SemaphoreType.DMA
     nz = n // 2
     buffer, basis, right, factor = pl.pallas_call(
         functools.partial(main_kernel, n, m),
         out_shape=(sds(rows, wide), sds(rows, rank), sds(wide, rank), sds(8, rank)),
-        in_specs=[vm] * 4,
-        out_specs=(vm,) * 4,
+        in_specs=[vm, vm, hbm, hbm],
+        out_specs=(hbm, vm, vm, vm),
         scratch_shapes=[
+            pltpu.VMEM((rows, wide), F32),
+            pltpu.VMEM((wide, rank), F32),
+            dma((3,)),
             pltpu.VMEM((rows, rank), F32),
             pltpu.VMEM((rank, rank), F32),
             pltpu.VMEM((wide, rank), F32),
@@ -334,7 +371,7 @@
             pltpu.VMEM((rank, 2 * rank), F32),
             pltpu.VMEM((m, 8, rank), F32),
             dma((m - 1,)), dma((m - 1,)),
-            pltpu.VMEM((n, tok, wide), F32),
+            pltpu.VMEM((n, CHUNKS, tok // CHUNKS, wide), F32),
             pltpu.VMEM((n, m, tok // m, rows), F32),
             pltpu.VMEM((n, tok // m, rows), F32),
             pltpu.VMEM((rows, n * tok), BF16),
@@ -344,7 +381,7 @@
             pltpu.VMEM((n, rank // m, rank), F32),
             pltpu.VMEM((wide, rank), F32),
             pltpu.VMEM((n - 1, wide // n, rank), F32),
-            dma((2, nz)), dma((nz,)), dma((nz,)), dma((nz,)),
+            dma((2, nz, CHUNKS)), dma((nz, CHUNKS)), dma((nz, CHUNKS)), dma((nz, CHUNKS)),
             dma((n - 1,)), dma((n - 1,)), dma((m - 1,)), dma((m - 1,)),
             dma((m - 1,)), dma((m - 1,)), dma((m - 1,)), dma((m - 1,)),
             dma((n - 1,)), dma((n - 1,)), dma((m - 1,)), dma((m - 1,)),

time: 197 us -> 181 us (0.919)
  Pallas kernels: 194 us -> 177 us
    pallas_call x1, Pallas kernels: 186 us -> 169 us  [kernels_on_device(): pl.pallas_call(functools.partial(main_kernel, n, m), out_shape=(sds(rows,...]
where the time goes in v3:
time: 181 us; the launch traced here: 179 us
  Pallas kernels  177 us (98%)
    pallas_call x1, Pallas kernels, kernels_on_device(): pl.pallas_call(functools.partial(main_kernel, n, m), out_shape=(sds(rows,...  169 us
    pallas_call x1, Pallas kernels, kernels_on_device(): pl.pallas_call(functools.partial(output_kernel, math.sqrt(size / rank)),...  8.22 us

profile of v3, /device:TPU:27, one launch (start us, length us, event | category | flops | bytes accessed | tf_op | source)
XLA Modules:
  0.0 179.3 jit_solution(524191657758982030)
XLA Ops:
  0.6 168.5 %shard_map.67 = (f32[640,1280]{1,0:T(8,128)}, f32[640,256]{1,0:T(8,128)}, f32[1280,256]{1,0:T(8,128)}, f32[8,256]{1,0:T(8,128)}) custom-call(bf16[128,1280]{1,0:T(8,128)(2,1)} %a_ref.1, bf16[128,5120]{1,0:T(8,128)(2,1)} %g_ref.1, f32[640,1280]{1,0:T(8,128)} %mom_ref.1, f32[1280,256]{1,0:T(8,128)} %p_hbm.1), custom_call_target="tpu_custom_call" | custom-call | tf_op jit(solution)/shard_map/pallas_call | solution.py:358
  169.2 0.0 copy-start
  169.2 8.2 %shard_map.68 = (f32[640,1280]{1,0:T(8,128)}, f32[640,1280]{1,0:T(8,128)}) custom-call(f32[640,1280]{1,0:T(8,128)} %get-tuple-element.9.buf_ref, f32[640,256]{1,0:T(8,128)} %get-tuple-element.10.basis_ref, f32[1280,256]{1,0:T(8,128)} %get-tuple-element.11.right_ref, f32[8,256]{1,0:T(8,128)} %get-tuple-element.12.factor_ref), custom_call_target="tpu_custom_call" | custom-call | tf_op jit(solution)/shard_map/pallas_call | solution.py:395
  177.4 0.7 slice.3
  178.1 0.1 dynamic-slice_bitcast_fusion
  178.2 0.0 copy-done
  178.2 0.2 dynamic-slice_multiply_fusion
  178.4 0.9 copy.7
Async XLA Ops:
  169.2 9.0 %copy-start = (f32[1280,256]{1,0:T(8,128)S(1)}, f32[1280,256]{1,0:T(8,128)}, u32[]{:S(2)}) copy-start(f32[1280,256]{1,0:T(8,128)} %get-tuple-element.11.right_ref) | copy-start | bytes 3932164
